TPU v7x, 256 devices: a whole 4x4x8 slice. The times are simulated.
256 devices in a mesh: dom: 16 (over z, core), tile: 16 (over x, y).
Axes of the slice: x: 4, y: 4, z: 8, core: 2. Of those that a mesh axis runs over, the one named last changes fastest.
Arguments:
- members: float32 [256, 4, 128, 384], P('dom', None, 'tile'), may hold values from -6 to 6
- noise: float32 [2, 256, 4, 128, 384], P(None, 'dom', None, 'tile'), may hold values from -4 to 4
- courant: float32 [2, 128, 384], P(None, 'tile'), may hold values from -0.35 to 0.35
- diffusion: float32 [4, 128, 384], P(None, 'tile'), may hold values from 0.02 to 0.07
- obs_loc: int32 [16, 64], P('tile'), may hold values from 0 to 3071
- observed: float32 [2, 16, 64], P(None, 'tile'), may hold values from -6 to 6
- obs_var: float32 [16, 64], P('tile'), may hold values from 0.1 to 1
- ancestors: int32 [2, 16, 256], P(None, 'tile'), may hold values from 0 to 255, as said below
Outputs:
- ensemble: float32 [256, 4, 128, 384], P('dom', None, 'tile')
- averages: float32 [2, 4, 128, 384], P(None, None, 'tile')
Inputs may be any that keep to these rules, and one draw needn't show every extreme that they name: `ancestors`: for every cycle, tile and group of 16 consecutive new particles, at most 2 of them descend from particles of one group of 16 consecutive old particles, and some group of old particles gives exactly 2.
All inputs are finite; a program needn't handle non-finite values.
Results may differ from a plain program's by a relative error of at most 0.0003.
Values sent between devices are 32-bit elements; how exact they have to be, the bound alone decides.
A program may use at most 64 MiB of HBM per device.

v0:
```python
import jax
import jax.numpy as jnp
from jax import lax
from jax.sharding import PartitionSpec as P

STEPS = 4
CYCLES = 2


def padded_2(block, sides, width):
    for axis, dim in sides:
        count = lax.axis_size(axis)
        forward = [(i, i + 1) for i in range(count - 1)]
        backward = [(target, source) for source, target in forward]
        low = lax.ppermute(
            lax.slice_in_dim(block, block.shape[dim] - width, None, axis=dim), axis, forward
        )
        high = lax.ppermute(lax.slice_in_dim(block, 0, width, axis=dim), axis, backward)
        block = jnp.concatenate([low, block, high], axis=dim)
    return block


def advance(current, coefficients, row_start, row_total):
    padded = jnp.pad(current, ((0, 0), (0, 0), (0, 0), (1, 1)))
    northern = padded[:, :, :-2, 1:-1]
    southern = padded[:, :, 2:, 1:-1]
    centre = padded[:, :, 1:-1, 1:-1]
    western = padded[:, :, 1:-1, :-2]
    eastern = padded[:, :, 1:-1, 2:]
    along_x = coefficients[0]
    along_y = coefficients[1]
    diffusion = coefficients[2:]
    transport = (
        jnp.maximum(along_x, 0.0) * (centre - northern)
        + jnp.minimum(along_x, 0.0) * (southern - centre)
        + jnp.maximum(along_y, 0.0) * (centre - western)
        + jnp.minimum(along_y, 0.0) * (eastern - centre)
    )
    laplace_sum = northern + southern + western + eastern - 4.0 * centre
    result = centre - transport + diffusion * laplace_sum
    row_number = row_start + jnp.arange(result.shape[2], dtype=jnp.int32)
    inside = (row_number >= 0) & (row_number < row_total)
    return jnp.where(inside[:, None], result, 0.0)


def per_device(members, noise, courant, diffusion, obs_loc, observed, obs_var, ancestors):
    per_group = members.shape[0]
    row_count = members.shape[2]
    groups = lax.axis_size("dom")
    group_index = lax.axis_index("dom")
    row_total = row_count * lax.axis_size("tile")
    first_row = lax.axis_index("tile") * row_count
    coefficients = jnp.concatenate([courant, diffusion], axis=0)
    fields = members
    averages = []
    for cycle_index in range(CYCLES):
        fields = fields + noise[cycle_index]
        for step_index in range(STEPS):
            current = padded_2(fields, (("tile", 2),), 1)
            fields = advance(current, coefficients, first_row, row_total)
        first_field = fields[:, 0].reshape(per_group, row_count * fields.shape[3])
        predicted = first_field[:, obs_loc[0]]
        misfit = observed[cycle_index, 0][None] - predicted
        log_likelihood = -0.5 * jnp.sum(misfit * misfit / obs_var[0][None], axis=1)
        peak_value = lax.pmax(jnp.max(log_likelihood), "dom")
        weight_total = lax.psum(jnp.sum(jnp.exp(log_likelihood - peak_value)), "dom")
        weight = jnp.exp(log_likelihood - peak_value) / weight_total
        local_average = jnp.einsum("p,pfrc->frc", weight, fields, precision=lax.Precision.HIGHEST)
        averages.append(lax.psum(local_average, "dom"))
        lineage = ancestors[cycle_index, 0].reshape(groups, per_group)
        gathered = lax.all_gather(fields, "dom", axis=0, tiled=True)
        mine_lineage = lax.dynamic_index_in_dim(lineage, group_index, 0, keepdims=False)
        fields = gathered[mine_lineage]
    return (fields, jnp.stack(averages))


def solution(mesh):
    return jax.shard_map(
        per_device,
        mesh=mesh,
        in_specs=(
            P("dom", None, "tile", None),
            P(None, "dom", None, "tile", None),
            P(None, "tile", None),
            P(None, "tile", None),
            P("tile", None),
            P(None, "tile", None),
            P("tile", None),
            P(None, "tile", None),
        ),
        out_specs=(P("dom", None, "tile", None), P(None, None, "tile", None)),
        check_vma=False,
    )
```

profile of v0, /device:TPU:1, one launch (start us, length us, event | category | flops | bytes accessed | tf_op | source)
XLA Modules:
  0.0 452.6 jit_solution(12337764362027988317)
XLA Ops:
  7.2 1.5 bitcast_add_fusion.1
  8.8 4.0 collective-permute-start
  12.9 1.3 collective-permute-start.1
  14.5 3.7 collective-permute-done.1
  18.2 1.3 select_maximum_fusion.14
  19.6 1.0 fusion.113
  20.7 3.2 collective-permute-start.2
  23.9 1.3 collective-permute-start.3
  25.6 3.7 collective-permute-done.3
  29.3 1.4 select_maximum_fusion.12
  31.8 4.4 collective-permute-start.4
  36.2 1.3 collective-permute-start.5
  37.9 3.7 collective-permute-done.5
  41.6 1.4 select_maximum_fusion.10
  44.1 4.0 collective-permute-start.6
  48.1 1.3 collective-permute-start.7
  49.7 4.0 collective-permute-done.7
  53.7 1.4 select_maximum_fusion.8
  55.1 1.9 fusion.68
  57.2 85.3 %all-gather.3.cloned.1.call-done = f32[256,4,8,384]{3,2,1,0:T(8,128)} async-done(((f32[16,4,8,384]{3,2,1,0:T(8,128)}), f32[256,4,8,384]{3,2,1,0:T(8,128)}) %all-gather.3.cloned.1.call-update) | async-done | bytes 12582928 | tf_op jit(solution)/shard_map/all_gather | solution.py:71
  142.5 5.2 %gather_fusion = f32[16,4,8,384]{3,2,1,0:T(8,128)S(1)} fusion(f32[256,4,8,384]{3,2,1,0:T(8,128)} %all-gather.3.cloned.1.call-done, s32[1024]{0:T(1024)S(1)} %pad_clamp_fusion.2), kind=kCustom, calls=%fused_computation | custom fusion | bytes 1572928 | tf_op jit(solution)/shard_map/gather | solution.py:73
  147.9 3.1 collective-permute-start.8
  151.0 1.5 collective-permute-start.9
  152.9 3.8 collective-permute-done.9
  156.7 1.4 select_maximum_fusion.6
  159.2 3.1 collective-permute-start.10
  162.4 1.3 collective-permute-start.11
  164.0 3.7 collective-permute-done.11
  167.7 1.4 select_maximum_fusion.4
  169.1 1.0 fusion.38
  170.2 4.6 %collective-permute-start.12 = (f32[16,4,1,384]{3,2,1,0:T(1,128)S(1)}, f32[16,4,1,384]{3,2,1,0:T(1,128)S(1)}, u32[]{:S(2)}, u32[]{:S(2)}) collective-permute-start(f32[16,4,1,384]{3,2,1,0:T(1,128)S(1)} %get-tuple-element.14), channel_id=1, source_target_pairs={{0,1},{1,2},{2,3},{3,4},{4,5},{5,6},{6,7},{7,8},{8,9},{9,10},{10,1... | collective-permute-start | bytes 294920 | tf_op jit(solution)/shard_map/ppermute | solution.py:15
  174.8 1.3 collective-permute-start.13
  176.5 3.7 collective-permute-done.13
  180.2 1.4 select_maximum_fusion.2
  182.7 4.0 collective-permute-start.14
  186.8 1.3 collective-permute-start.15
  188.1 1.7 copy.14
  189.8 2.0 gather_fusion.2
  192.1 1.3 select_maximum_fusion
  197.0 28.7 %all-reduce.10 = (f32[]{:T(128)}, f32[]{:T(128)}) all-reduce(f32[]{:T(128)} %multiply_reduce_fusion, f32[]{:T(128)} %multiply_reduce_fusion.1), channel_id=1, replica_groups=mesh['dom'=16,'tile'=16] {'dom'}, use_global_device_ids=true, to_apply=%region_8.9 | all-reduce | flops 2 | bytes 16 | tf_op jit(solution)/shard_map/pmax | solution.py:65
  225.6 1.9 fusion.136
  227.5 24.2 %all-reduce.9 = (f32[]{:T(128)}, f32[]{:T(128)}) all-reduce(f32[]{:T(128)} %get-tuple-element.35, f32[]{:T(128)} %get-tuple-element.34), channel_id=1, replica_groups=mesh['dom'=16,'tile'=16] {'dom'}, use_global_device_ids=true, to_apply=%region_10.11 | all-reduce | flops 2 | bytes 16 | tf_op jit(solution)/shard_map/psum | solution.py:66
  251.8 2.2 fusion.123
  254.6 2.2 fusion.121
  258.4 103.2 %all-reduce.13.cloned.1.call-done = (f32[1,4,8,384]{3,2,1,0:T(8,128)}, f32[1,4,8,384]{3,2,1,0:T(8,128)}) async-done(((f32[1,4,8,384]{3,2,1,0:T(8,128)}, f32[1,4,8,384]{3,2,1,0:T(8,128)}), (f32[1,4,8,384]{3,2,1,0:T(8,128)}, f32[1,4,8,384]{3,2,1,0:T(8,128)})) %all-reduce.13.cloned.1.call-update) | async-done | bytes 98320 | tf_op jit(solution)/shard_map/psum | solution.py:69
  361.6 1.5 pad_maximum_fusion.16
  363.0 77.0 %all-gather.5.cloned.1.call-done = f32[256,4,8,384]{3,2,1,0:T(8,128)} async-done(((f32[16,4,8,384]{3,2,1,0:T(8,128)}), f32[256,4,8,384]{3,2,1,0:T(8,128)}) %all-gather.5.cloned.1.call-update) | async-done | bytes 12582928 | tf_op jit(solution)/shard_map/all_gather | solution.py:71
  440.1 6.0 %gather_fusion.1 = f32[16,4,8,384]{3,2,1,0:T(8,128)} fusion(f32[256,4,8,384]{3,2,1,0:T(8,128)} %all-gather.5.cloned.1.call-done, s32[1024]{0:T(1024)S(1)} %pad_clamp_fusion.1), kind=kCustom, calls=%fused_computation.1 | custom fusion | bytes 1572928 | tf_op jit(solution)/shard_map/gather | solution.py:73
  (68 shorter events, 13.4 us)
Async XLA Ops:
  7.2 7.0 %copy-start.4 = (f32[2,8,384]{2,1,0:T(8,128)S(1)}, f32[2,8,384]{2,1,0:T(8,128)}, u32[]{:S(2)}) copy-start(f32[2,8,384]{2,1,0:T(8,128)} %param.10) | copy-start | bytes 73732
  7.2 135.3 %all-gather.3.cloned.1.call-start = ((), (), s32[]{:S(2)}) async-start(), calls=%async_computation | async-start | bytes 13369344 | tf_op jit(solution)/shard_map/all_gather | solution.py:71
  8.7 10.9 %copy-start.2 = (f32[4,8,384]{2,1,0:T(8,128)S(1)}, f32[4,8,384]{2,1,0:T(8,128)}, u32[]{:S(2)}) copy-start(f32[4,8,384]{2,1,0:T(8,128)} %param.11) | copy-start | bytes 147460
  8.8 5.7 %collective-permute-start = (f32[16,4,1,384]{3,2,1,0:T(1,128)S(1)}, f32[16,4,1,384]{3,2,1,0:T(1,128)S(1)}, u32[]{:S(2)}, u32[]{:S(2)}) collective-permute-start(f32[16,4,1,384]{3,2,1,0:T(1,128)S(1)} %get-tuple-element.26), channel_id=1, source_target_pairs={{0,1},{1,2},{2,3},{3,4},{4,5},{5,6},{6,7},{7,8},{8,9},{9,10},{10,1... | collective-permute-start | bytes 294920 | tf_op jit(solution)/shard_map/ppermute | solution.py:15
  12.9 5.4 %collective-permute-start.1 = (f32[16,4,1,384]{3,2,1,0:T(1,128)S(1)}, f32[16,4,1,384]{3,2,1,0:T(1,128)S(1)}, u32[]{:S(2)}, u32[]{:S(2)}) collective-permute-start(f32[16,4,1,384]{3,2,1,0:T(1,128)S(1)} %get-tuple-element.27), channel_id=1, source_target_pairs={{1,0},{2,1},{3,2},{4,3},{5,4},{6,5},{7,6},{8,7},{9,8},{10,9},{11,1... | collective-permute-start | bytes 294920 | tf_op jit(solution)/shard_map/ppermute | solution.py:18
  20.7 4.8 %collective-permute-start.2 = (f32[16,4,1,384]{3,2,1,0:T(1,128)S(1)}, f32[16,4,1,384]{3,2,1,0:T(1,128)S(1)}, u32[]{:S(2)}, u32[]{:S(2)}) collective-permute-start(f32[16,4,1,384]{3,2,1,0:T(1,128)S(1)} %get-tuple-element.24), channel_id=1, source_target_pairs={{0,1},{1,2},{2,3},{3,4},{4,5},{5,6},{6,7},{7,8},{8,9},{9,10},{10,1... | collective-permute-start | bytes 294920 | tf_op jit(solution)/shard_map/ppermute | solution.py:15
  23.9 5.4 %collective-permute-start.3 = (f32[16,4,1,384]{3,2,1,0:T(1,128)S(1)}, f32[16,4,1,384]{3,2,1,0:T(1,128)S(1)}, u32[]{:S(2)}, u32[]{:S(2)}) collective-permute-start(f32[16,4,1,384]{3,2,1,0:T(1,128)S(1)} %get-tuple-element.25), channel_id=1, source_target_pairs={{1,0},{2,1},{3,2},{4,3},{5,4},{6,5},{7,6},{8,7},{9,8},{10,9},{11,1... | collective-permute-start | bytes 294920 | tf_op jit(solution)/shard_map/ppermute | solution.py:18
  31.8 6.1 %collective-permute-start.4 = (f32[16,4,1,384]{3,2,1,0:T(1,128)S(1)}, f32[16,4,1,384]{3,2,1,0:T(1,128)S(1)}, u32[]{:S(2)}, u32[]{:S(2)}) collective-permute-start(f32[16,4,1,384]{3,2,1,0:T(1,128)S(1)} %get-tuple-element.22), channel_id=1, source_target_pairs={{0,1},{1,2},{2,3},{3,4},{4,5},{5,6},{6,7},{7,8},{8,9},{9,10},{10,1... | collective-permute-start | bytes 294920 | tf_op jit(solution)/shard_map/ppermute | solution.py:15
  36.2 5.4 %collective-permute-start.5 = (f32[16,4,1,384]{3,2,1,0:T(1,128)S(1)}, f32[16,4,1,384]{3,2,1,0:T(1,128)S(1)}, u32[]{:S(2)}, u32[]{:S(2)}) collective-permute-start(f32[16,4,1,384]{3,2,1,0:T(1,128)S(1)} %get-tuple-element.23), channel_id=1, source_target_pairs={{1,0},{2,1},{3,2},{4,3},{5,4},{6,5},{7,6},{8,7},{9,8},{10,9},{11,1... | collective-permute-start | bytes 294920 | tf_op jit(solution)/shard_map/ppermute | solution.py:18
  44.1 5.7 %collective-permute-start.6 = (f32[16,4,1,384]{3,2,1,0:T(1,128)S(1)}, f32[16,4,1,384]{3,2,1,0:T(1,128)S(1)}, u32[]{:S(2)}, u32[]{:S(2)}) collective-permute-start(f32[16,4,1,384]{3,2,1,0:T(1,128)S(1)} %get-tuple-element.20), channel_id=1, source_target_pairs={{0,1},{1,2},{2,3},{3,4},{4,5},{5,6},{6,7},{7,8},{8,9},{9,10},{10,1... | collective-permute-start | bytes 294920 | tf_op jit(solution)/shard_map/ppermute | solution.py:15
  48.1 5.6 %collective-permute-start.7 = (f32[16,4,1,384]{3,2,1,0:T(1,128)S(1)}, f32[16,4,1,384]{3,2,1,0:T(1,128)S(1)}, u32[]{:S(2)}, u32[]{:S(2)}) collective-permute-start(f32[16,4,1,384]{3,2,1,0:T(1,128)S(1)} %get-tuple-element.21), channel_id=1, source_target_pairs={{1,0},{2,1},{3,2},{4,3},{5,4},{6,5},{7,6},{8,7},{9,8},{10,9},{11,1... | collective-permute-start | bytes 294920 | tf_op jit(solution)/shard_map/ppermute | solution.py:18
  55.1 2.0 copy-start.5
  55.1 92.5 %copy-start.3 = (f32[2,16,4,8,384]{4,3,2,1,0:T(8,128)S(1)}, f32[2,16,4,8,384]{4,3,2,1,0:T(8,128)}, u32[]{:S(2)}) copy-start(f32[2,16,4,8,384]{4,3,2,1,0:T(8,128)} %param.9) | copy-start | bytes 4718596
  57.0 304.6 %all-reduce.13.cloned.1.call-start = ((), (), s32[]{:S(2)}) async-start(), calls=%async_computation.2 | async-start | bytes 196608 | tf_op jit(solution)/shard_map/psum | solution.py:69
  147.9 5.0 %collective-permute-start.8 = (f32[16,4,1,384]{3,2,1,0:T(1,128)S(1)}, f32[16,4,1,384]{3,2,1,0:T(1,128)S(1)}, u32[]{:S(2)}, u32[]{:S(2)}) collective-permute-start(f32[16,4,1,384]{3,2,1,0:T(1,128)S(1)} %get-tuple-element.18), channel_id=1, source_target_pairs={{0,1},{1,2},{2,3},{3,4},{4,5},{5,6},{6,7},{7,8},{8,9},{9,10},{10,1... | collective-permute-start | bytes 294920 | tf_op jit(solution)/shard_map/ppermute | solution.py:15
  151.0 5.7 %collective-permute-start.9 = (f32[16,4,1,384]{3,2,1,0:T(1,128)S(1)}, f32[16,4,1,384]{3,2,1,0:T(1,128)S(1)}, u32[]{:S(2)}, u32[]{:S(2)}) collective-permute-start(f32[16,4,1,384]{3,2,1,0:T(1,128)S(1)} %get-tuple-element.19), channel_id=1, source_target_pairs={{1,0},{2,1},{3,2},{4,3},{5,4},{6,5},{7,6},{8,7},{9,8},{10,9},{11,1... | collective-permute-start | bytes 294920 | tf_op jit(solution)/shard_map/ppermute | solution.py:18
  158.1 5.5 %copy-start.6 = (f32[2,1,64]{2,1,0:T(1,128)S(1)}, f32[2,1,64]{2,1,0:T(1,128)}, u32[]{:S(2)}) copy-start(f32[2,1,64]{2,1,0:T(1,128)} %param.13) | copy-start | bytes 1540
  159.2 4.7 %collective-permute-start.10 = (f32[16,4,1,384]{3,2,1,0:T(1,128)S(1)}, f32[16,4,1,384]{3,2,1,0:T(1,128)S(1)}, u32[]{:S(2)}, u32[]{:S(2)}) collective-permute-start(f32[16,4,1,384]{3,2,1,0:T(1,128)S(1)} %get-tuple-element.16), channel_id=1, source_target_pairs={{0,1},{1,2},{2,3},{3,4},{4,5},{5,6},{6,7},{7,8},{8,9},{9,10},{10,1... | collective-permute-start | bytes 294920 | tf_op jit(solution)/shard_map/ppermute | solution.py:15
  162.4 5.4 %collective-permute-start.11 = (f32[16,4,1,384]{3,2,1,0:T(1,128)S(1)}, f32[16,4,1,384]{3,2,1,0:T(1,128)S(1)}, u32[]{:S(2)}, u32[]{:S(2)}) collective-permute-start(f32[16,4,1,384]{3,2,1,0:T(1,128)S(1)} %get-tuple-element.17), channel_id=1, source_target_pairs={{1,0},{2,1},{3,2},{4,3},{5,4},{6,5},{7,6},{8,7},{9,8},{10,9},{11,1... | collective-permute-start | bytes 294920 | tf_op jit(solution)/shard_map/ppermute | solution.py:18
  169.1 7.1 %copy-start.8 = (s32[1,64]{1,0:T(1,128)S(1)}, s32[1,64]{1,0:T(1,128)}, u32[]{:S(2)}) copy-start(s32[1,64]{1,0:T(1,128)} %param.12) | copy-start | bytes 772
  170.2 6.2 %collective-permute-start.12 = (f32[16,4,1,384]{3,2,1,0:T(1,128)S(1)}, f32[16,4,1,384]{3,2,1,0:T(1,128)S(1)}, u32[]{:S(2)}, u32[]{:S(2)}) collective-permute-start(f32[16,4,1,384]{3,2,1,0:T(1,128)S(1)} %get-tuple-element.14), channel_id=1, source_target_pairs={{0,1},{1,2},{2,3},{3,4},{4,5},{5,6},{6,7},{7,8},{8,9},{9,10},{10,1... | collective-permute-start | bytes 294920 | tf_op jit(solution)/shard_map/ppermute | solution.py:15
  174.8 5.4 %collective-permute-start.13 = (f32[16,4,1,384]{3,2,1,0:T(1,128)S(1)}, f32[16,4,1,384]{3,2,1,0:T(1,128)S(1)}, u32[]{:S(2)}, u32[]{:S(2)}) collective-permute-start(f32[16,4,1,384]{3,2,1,0:T(1,128)S(1)} %get-tuple-element.15), channel_id=1, source_target_pairs={{1,0},{2,1},{3,2},{4,3},{5,4},{6,5},{7,6},{8,7},{9,8},{10,9},{11,1... | collective-permute-start | bytes 294920 | tf_op jit(solution)/shard_map/ppermute | solution.py:18
  181.6 6.5 %copy-start = (f32[16,4,8,384]{3,2,1,0:T(8,128)S(1)}, f32[16,4,8,384]{3,2,1,0:T(8,128)}, u32[]{:S(2)}) copy-start(f32[16,4,8,384]{3,2,1,0:T(8,128)} %fusion.68) | copy-start | bytes 2359300
  182.7 9.1 %collective-permute-start.14 = (f32[16,4,1,384]{3,2,1,0:T(1,128)S(1)}, f32[16,4,1,384]{3,2,1,0:T(1,128)S(1)}, u32[]{:S(2)}, u32[]{:S(2)}) collective-permute-start(f32[16,4,1,384]{3,2,1,0:T(1,128)S(1)} %get-tuple-element.12), channel_id=1, source_target_pairs={{0,1},{1,2},{2,3},{3,4},{4,5},{5,6},{6,7},{7,8},{8,9},{9,10},{10,1... | collective-permute-start | bytes 294920 | tf_op jit(solution)/shard_map/ppermute | solution.py:15
  186.8 5.4 %collective-permute-start.15 = (f32[16,4,1,384]{3,2,1,0:T(1,128)S(1)}, f32[16,4,1,384]{3,2,1,0:T(1,128)S(1)}, u32[]{:S(2)}, u32[]{:S(2)}) collective-permute-start(f32[16,4,1,384]{3,2,1,0:T(1,128)S(1)} %get-tuple-element.13), channel_id=1, source_target_pairs={{1,0},{2,1},{3,2},{4,3},{5,4},{6,5},{7,6},{8,7},{9,8},{10,9},{11,1... | collective-permute-start | bytes 294920 | tf_op jit(solution)/shard_map/ppermute | solution.py:18
  193.5 2.1 copy-start.7
  194.5 63.0 %copy-start.1 = (f32[16,4,8,384]{3,2,1,0:T(8,128)}, f32[16,4,8,384]{3,2,1,0:T(8,128)S(1)}, u32[]{:S(2)}) copy-start(f32[16,4,8,384]{3,2,1,0:T(8,128)S(1)} %fusion.8) | copy-start | bytes 2359300
  257.5 182.6 %all-gather.5.cloned.1.call-start = ((), (), s32[]{:S(2)}) async-start(), calls=%async_computation.1 | async-start | bytes 13369344 | tf_op jit(solution)/shard_map/all_gather | solution.py:71
Sparse Core Ops, SparseCore 0:
  57.1 85.2 all-gather.2
  257.6 103.8 all-reduce.12
  364.1 75.8 all-gather.4
where the time goes:
time: 453 us
  waiting for transfers between devices  295 us (65%)
  blocking collectives  52.9 us (12%)
  starting transfers between devices  41.2 us (9%)
  other arithmetic  26 us (6%)
  local copies, waits for them, and re-layouts  18.4 us (4%)
  between operations  14.3 us (3%)
    all_gather x2, waiting for transfers between devices, per_device(): gathered = lax.all_gather(fields, 'dom', axis=0, tiled=True)  162 us
    psum x1, waiting for transfers between devices, per_device(): averages.append(lax.psum(local_average, 'dom'))  103 us
    ppermute x8, starting transfers between devices, padded_2(): lax.ppermute(lax.slice_in_dim(block, block.shape[dim] - width, None, axis...  30.6 us
    pmax x1, blocking collectives, per_device(): peak_value = lax.pmax(jnp.max(log_likelihood), 'dom')  28.7 us
    ppermute x8, waiting for transfers between devices, padded_2(): lax.ppermute(lax.slice_in_dim(block, 0, width, axis=dim), axis, backward)  26.9 us
    psum x1, blocking collectives, per_device(): lax.psum(jnp.sum(jnp.exp(log_likelihood - peak_value)), 'dom')  24.2 us
    gather x2, local copies, waits for them, and re-layouts, per_device(): fields = gathered[mine_lineage]  11.2 us
    concatenate x8, other arithmetic, padded_2(): block = jnp.concatenate([low, block, high], axis=dim)  10.9 us
  transfers between devices with their start and end apart: 19, of which 18 were waited for; matrix products, arithmetic and copies ran while one was open for 1% of the time, Pallas kernels for 0%

commit v1 on v0

v1 whole, which is shorter than its diff:
```python
import jax
import jax.numpy as jnp
from jax import lax
from jax.experimental import pallas as pl
from jax.experimental.pallas import tpu as pltpu
from jax.sharding import PartitionSpec as P

MESH = pl.DeviceIdType.MESH
STEPS = 4
CYCLES = 2
FIELDS = 4
PER = 16
GROUPS = 16
ALL = PER * GROUPS
PAIRS = ALL // 2
TILES = 16
ROWS = 8
COLS = 384
LANES = 128
HALF = LANES // 2
NOBS = 64
CHUNKS = 2
PAIR = 2
STRIPS = 8
WIDE = COLS // STRIPS
EDGE = STEPS
SPAN = WIDE + 2 * EDGE
BLOCKS = 4
BLOCK = PAIRS // 2 // BLOCKS


def half_turn(x):
    return pltpu.roll(x, 4, axis=0)


def place(vector, spans, rows=ROWS):
    lane = lax.broadcasted_iota(jnp.int32, (rows, LANES), 1)
    result = None
    for begin, column, length, load, limit in spans:
        low, high = max(begin, vector * LANES), min(begin + length, (vector + 1) * LANES)
        if low >= high:
            continue
        column = column + low - begin
        low, high = low - vector * LANES, high - vector * LANES
        first = max(column, 0) // LANES
        last = min(column + high - low, limit) - 1
        for u in range(first, last // LANES + 1):
            piece = load(u)
            shift = (low - column + LANES * u) % LANES
            if shift:
                piece = pltpu.roll(piece, shift, axis=1)
            start = max(low, low - column + LANES * u)
            result = piece if result is None else jnp.where(lane >= start, piece, result)
    return result


def kernel(members, noise, courant, diffusion, obs_loc, observed, obs_var, ancestors, out, averages,
           members_v, noise_v, courant_v, diffusion_v, obs_loc_s, observed_s, obs_var_s, ancestors_s, out_v,
           noise_send, noise_recv, state_send, state_recv, back_send, back_recv,
           to_north, to_south, from_north, from_south, to_north2, to_south2, from_north2, from_south2,
           state, result, raw, raw_north, raw_south, coef, obs_weight, obs_mean, obs_rest, partial, likely, weights,
           like_send, like_recv, part_send, part_recv, mean_send, mean_recv,
           noise_pairs, twins, state2, lone, coef2, windows, obs2, cost2, like2, weights2, like_send2, like_recv2,
           mean_send2, mean_recv2,
           sem_load, sem_store, sem_out, sem_in, sem_halo_out, sem_halo_in, sem_halo2_out, sem_halo2_in, sem_raw_out,
           sem_raw_in, sem_small_out, sem_small_in):
    me = lax.axis_index("dom")
    tile = lax.axis_index("tile")
    north = lax.rem(tile + TILES - 1, TILES)
    south = lax.rem(tile + 1, TILES)
    strip = lax.rem(me, STRIPS)
    in_pair = lax.div(me, STRIPS)

    def peer(step):
        return lax.rem(me + step, GROUPS)

    barrier = pltpu.get_barrier_semaphore()

    def greet(step, carry):
        pl.semaphore_signal(barrier, inc=1, device_id={"dom": peer(step)}, device_id_type=MESH)
        return carry

    for neighbour in (north, south):
        pl.semaphore_signal(barrier, inc=1, device_id={"tile": neighbour}, device_id_type=MESH)
    lax.fori_loop(1, GROUPS, greet, 0)

    loads = []

    def load(source, target):
        loads.append(pltpu.make_async_copy(source, target, sem_load.at[len(loads)]))
        loads[-1].start()

    for chunk in range(CHUNKS):
        two = pl.ds(PAIR * chunk, PAIR)
        load(members.at[:, two], members_v.at[:, two])
        load(noise.at[0, :, two], noise_v.at[0, :, two])
        load(noise.at[1, :, two], noise_v.at[1, :, two])
    for source, target in ((courant, courant_v), (diffusion, diffusion_v), (obs_loc, obs_loc_s),
                           (observed, observed_s), (obs_var, obs_var_s), (ancestors, ancestors_s)):
        load(source, target)

    upper = lax.broadcasted_iota(jnp.int32, (ROWS, COLS), 0) < 4
    upper1 = lax.broadcasted_iota(jnp.int32, (ROWS, LANES), 0) < 4
    column = lax.broadcasted_iota(jnp.int32, (ROWS, COLS), 1)
    lane8 = lax.broadcasted_iota(jnp.int32, (ROWS, LANES), 1)
    has_north = jnp.where(tile > 0, 1.0, 0.0).astype(jnp.float32)
    has_south = jnp.where(tile < TILES - 1, 1.0, 0.0).astype(jnp.float32)

    def exchange(source_of, target_of, out_sem, in_sem):
        def one(step, carry):
            other = peer(step)
            pltpu.make_async_remote_copy(
                src_ref=source_of(other), dst_ref=target_of(me), send_sem=out_sem, recv_sem=in_sem,
                device_id={"dom": other}, device_id_type=MESH,
            ).start()
            return carry

        lax.fori_loop(1, GROUPS, one, 0)

    def await_bytes(ref, sem):
        pltpu.make_async_copy(ref, ref, sem).wait()

    def others(ref, chunk):
        return ref.at[chunk, pl.ds(0, GROUPS - 1)]

    def tile_copy(source, target, out_sem, in_sem, southward):
        return pltpu.make_async_remote_copy(
            src_ref=source, dst_ref=target, send_sem=out_sem, recv_sem=in_sem,
            device_id={"tile": south if southward else north}, device_id_type=MESH,
        )

    def halo_copy(field, southward):
        source, target = (to_south, from_north) if southward else (to_north, from_south)
        way = 1 if southward else 0
        return tile_copy(source.at[field], target.at[field], sem_halo_out.at[field, way], sem_halo_in.at[field, way],
                         southward)

    def halo_copy2(chunk, block, southward):
        source, target = (to_south2, from_north2) if southward else (to_north2, from_south2)
        way = 1 if southward else 0
        rows = pl.ds(BLOCK * block, BLOCK)
        return tile_copy(source.at[chunk, rows], target.at[chunk, rows], sem_halo2_out.at[chunk, block, way],
                         sem_halo2_in.at[chunk, block, way], southward)

    def raw_copy(part, southward):
        rows = pl.ds(3 * part, 3)
        target = raw_north if southward else raw_south
        way = 1 if southward else 0
        return tile_copy(raw.at[rows], target.at[rows], sem_raw_out.at[part, way], sem_raw_in.at[part, way], southward)

    def begin(field):
        def pair(i, carry):
            first, second = 2 * i, 2 * i + 1
            v0 = members_v[first, field] + noise_v[0, first, field]
            v1 = members_v[second, field] + noise_v[0, second, field]
            r0, r1 = half_turn(v0), half_turn(v1)
            state[field, first] = r0
            state[field, second] = r1
            to_south[field, i] = jnp.where(upper, r0, v1)
            to_north[field, i] = jnp.where(upper, v0, r1)
            return carry

        lax.fori_loop(0, PER // 2, pair, 0, unroll=2)

    def march(x, c):
        width = x.shape[1]
        for _ in range(STEPS):
            x = (c(0) * x + c(1) * pltpu.roll(x, 1, axis=0) + c(2) * pltpu.roll(x, 2 * ROWS - 1, axis=0)
                 + c(3) * pltpu.roll(x, 1, axis=1) + c(4) * pltpu.roll(x, width - 1, axis=1))
        return x

    def forecast(field):
        halo_copy(field, True).wait_recv()
        halo_copy(field, False).wait_recv()

        def pair(i, carry):
            top = from_north[field, i] * has_north
            bottom = from_south[field, i] * has_south
            for k, (above, below) in enumerate(((top, half_turn(bottom)), (half_turn(top), bottom))):
                particle = 2 * i + k
                r = state[field, particle]
                x = jnp.concatenate([jnp.where(upper, above, r), jnp.where(upper, r, below)], axis=0)
                x = march(x, lambda n: coef[field, n])
                v = half_turn(jnp.where(upper, x[ROWS:], x[:ROWS]))
                result[field, particle] = v
                if field == 0:
                    miss = v - obs_mean[0]
                    cost = obs_weight[...] * miss * miss + obs_rest[0]
                    cost = cost[:, :LANES] + cost[:, LANES:2 * LANES] + cost[:, 2 * LANES:]
                    partial[pl.ds(particle, 1), :] = jnp.sum(cost, axis=0, keepdims=True)
            return carry

        lax.fori_loop(0, PER // 2, pair, 0)

    def pack(chunk, get, outgoing, incoming):
        def one(f, carry):
            for g in range(STRIPS):
                def loader(k):
                    return lambda u: get(k, PAIR * chunk + f, pl.ds(LANES * u, LANES))

                spans = [(SPAN * k, WIDE * g - EDGE, SPAN, loader(k), COLS) for k in range(PER)]
                for j in range(PER * SPAN // LANES):
                    outgoing[chunk, STRIPS * f + g, :, LANES * j:LANES * (j + 1)] = place(j, spans)
            return carry

        lax.fori_loop(0, PAIR, one, 0)
        incoming[chunk, me] = outgoing[chunk, me]

    def swap(outgoing, incoming, chunk, which):
        exchange(lambda other: outgoing.at[chunk, other], lambda mine: incoming.at[chunk, mine],
                 sem_out.at[chunk, which], sem_in.at[chunk, which])

    def unpack_noise(chunk):
        await_bytes(others(noise_recv, chunk), sem_in.at[chunk, 0])

        def one(s, carry):
            def load_from(u):
                return noise_recv[chunk, s, :, LANES * u:LANES * (u + 1)]

            for m in range(PER // 2):
                noise_pairs[chunk, PER // 2 * s + m] = place(
                    0, [(HALF * h, SPAN * (2 * m + h), SPAN, load_from, PER * SPAN) for h in range(2)])
            return carry

        lax.fori_loop(0, GROUPS, one, 0)

    def unpack_state(chunk):

        def one(s, carry):
            def load_from(u):
                return state_recv[chunk, s, :, LANES * u:LANES * (u + 1)]

            for k in range(PER):
                twins[chunk, PER * s + k] = place(
                    0, [(HALF * h, SPAN * k, SPAN, load_from, PER * SPAN) for h in range(2)])
            return carry

        lax.fori_loop(0, GROUPS, one, 0)

    def begin2(chunk, block):
        left = lane8 < HALF

        def pair(i, carry):
            v = []
            for k in range(2):
                m = 2 * i + k
                old0, old1 = ancestors_s[0, 0, 2 * m], ancestors_s[0, 0, 2 * m + 1]
                v.append(jnp.where(left, twins[chunk, old0], twins[chunk, old1]) + noise_pairs[chunk, m])
            r0, r1 = half_turn(v[0]), half_turn(v[1])
            state2[chunk, 2 * i] = r0
            state2[chunk, 2 * i + 1] = r1
            to_south2[chunk, i] = jnp.where(upper1, r0, v[1])
            to_north2[chunk, i] = jnp.where(upper1, v[0], r1)
            return carry

        lax.fori_loop(BLOCK * block, BLOCK * (block + 1), pair, 0, unroll=4)
        halo_copy2(chunk, block, True).start()
        halo_copy2(chunk, block, False).start()

    def forecast2(chunk, block):
        halo_copy2(chunk, block, True).wait_recv()
        halo_copy2(chunk, block, False).wait_recv()

        def pair(i, carry):
            top = from_north2[chunk, i] * has_north
            bottom = from_south2[chunk, i] * has_south
            for k, (above, below) in enumerate(((top, half_turn(bottom)), (half_turn(top), bottom))):
                m = 2 * i + k
                r = state2[chunk, m]
                x = jnp.concatenate([jnp.where(upper1, above, r), jnp.where(upper1, r, below)], axis=0)
                x = march(x, lambda n: coef2[chunk, n])
                v = half_turn(jnp.where(upper1, x[ROWS:], x[:ROWS]))
                lone[chunk, 2 * m] = v
                lone[chunk, 2 * m + 1] = pltpu.roll(v, HALF, axis=1)
                if chunk == 0:
                    miss = v - obs2[1]
                    cost = obs2[0] * miss * miss + obs2[2]
                    cost2[pl.ds(m, 1), :] = jnp.sum(cost, axis=0, keepdims=True)
            return carry

        lax.fori_loop(BLOCK * block, BLOCK * (block + 1), pair, 0, unroll=2)

    def pack_back(chunk):
        def one(group, carry):
            def loader(j):
                old = ancestors_s[1, 0, PER * group + j]
                return lambda u: lone[chunk, old]

            spans = [(WIDE * j, EDGE, WIDE, loader(j), LANES) for j in range(PER)]
            for n in range(PER * WIDE // LANES):
                back_send[chunk, group, :, LANES * n:LANES * (n + 1)] = place(n, spans)
            return carry

        lax.fori_loop(0, GROUPS, one, 0)
        back_recv[chunk, me] = back_send[chunk, me]

    def store(chunk):
        two = pl.ds(PAIR * chunk, PAIR)
        return pltpu.make_async_copy(out_v.at[:, two], out.at[:, two], sem_store.at[chunk])

    def finish(chunk):
        await_bytes(others(back_recv, chunk), sem_in.at[chunk, 2])

        def one(f, carry):
            def loader(g):
                return lambda u: back_recv[chunk, STRIPS * f + g, :, LANES * u:LANES * (u + 1)]

            for j in range(PER):
                spans = [(WIDE * g, WIDE * j, WIDE, loader(g), PER * WIDE) for g in range(STRIPS)]
                for u in range(COLS // LANES):
                    out_v[j, PAIR * chunk + f, :, LANES * u:LANES * (u + 1)] = place(u, spans)
            return carry

        lax.fori_loop(0, PAIR, one, 0)
        store(chunk).start()

    lane = lax.broadcasted_iota(jnp.int32, (PER, LANES), 1)
    line = lax.broadcasted_iota(jnp.int32, (PER, LANES), 0)

    def likelihood():
        total = -0.5 * jnp.sum(partial[...], axis=1, keepdims=True)
        spread = jnp.broadcast_to(total, (PER, LANES))
        likely[...] = spread
        row = jnp.sum(jnp.where(lane == line, spread, 0.0), axis=0, keepdims=True)
        like_send[...] = row
        like_recv[me] = row
        exchange(lambda other: like_send, lambda mine: like_recv.at[mine], sem_small_out.at[0], sem_small_in.at[0])

    def weigh():
        await_bytes(like_recv.at[pl.ds(0, GROUPS - 1)], sem_small_in.at[0])
        everyone = like_recv[...]
        known = lax.broadcasted_iota(jnp.int32, (GROUPS, 1, LANES), 2) < PER
        peak = jnp.max(jnp.where(known, everyone, -3.0e38), axis=0)
        peak = jnp.max(peak, axis=1, keepdims=True)
        shifted = jnp.where(known, jnp.exp(jnp.where(known, everyone - peak[None], 0.0)), 0.0)
        total = jnp.sum(jnp.sum(shifted, axis=0), axis=1, keepdims=True)
        weights[...] = jnp.exp(likely[...] - peak) / total

    def average():
        def add(p, sums):
            w = weights[pl.ds(p, 1), :]
            w = jnp.concatenate([w, w, w], axis=1)
            return tuple(s + w * result[f, p] for f, s in enumerate(sums))

        sums = lax.fori_loop(0, PER, add, tuple(jnp.zeros((ROWS, COLS), jnp.float32) for _ in range(FIELDS)))
        for f in range(FIELDS):
            for k in range(4):
                part_send[4 * f + k] = sums[f][2 * k:2 * k + 2]
        part_recv[me] = part_send[me]
        exchange(lambda other: part_send.at[other], lambda mine: part_recv.at[mine], sem_small_out.at[1],
                 sem_small_in.at[1])

    def combine():
        await_bytes(part_recv.at[pl.ds(0, GROUPS - 1)], sem_small_in.at[1])
        total = part_recv[0]
        for g in range(1, GROUPS):
            total = total + part_recv[g]
        mean_send[...] = total
        mean_recv[me] = total
        exchange(lambda other: mean_send, lambda mine: mean_recv.at[mine], sem_small_out.at[2], sem_small_in.at[2])

    place2 = lax.broadcasted_iota(jnp.int32, (PAIRS, LANES), 1)
    line2 = lax.broadcasted_iota(jnp.int32, (PAIRS, LANES), 0)

    def likelihood2():
        cost = cost2[...]
        for h in range(2):
            side = (place2 < HALF) if h == 0 else (place2 >= HALF)
            total = -0.5 * jnp.sum(jnp.where(side, cost, 0.0), axis=1, keepdims=True)
            row = jnp.sum(jnp.where(place2 == line2, total, 0.0), axis=0, keepdims=True)
            like_send2[h:h + 1, :] = row
        like_recv2[me] = like_send2[...]
        exchange(lambda other: like_send2, lambda mine: like_recv2.at[mine], sem_small_out.at[3], sem_small_in.at[3])

    def weigh2():
        await_bytes(like_recv2.at[pl.ds(0, GROUPS - 1)], sem_small_in.at[3])
        total = like_recv2[0]
        for g in range(1, GROUPS):
            total = total + like_recv2[g]
        peak = jnp.max(jnp.max(total, axis=0, keepdims=True), axis=1, keepdims=True)
        shifted = jnp.exp(total - peak)
        weight = shifted / jnp.sum(jnp.sum(shifted, axis=0, keepdims=True), axis=1, keepdims=True)
        sides = [jnp.sum(jnp.where(place2 == line2, weight[h:h + 1], 0.0), axis=1, keepdims=True) for h in range(2)]
        weights2[...] = jnp.where(place2 < HALF, sides[0], sides[1])

    def average2(chunk):
        def add(m, total):
            return total + weights2[pl.ds(m, 1), :] * lone[chunk, 2 * m]

        total = lax.fori_loop(0, PAIRS, add, jnp.zeros((ROWS, LANES), jnp.float32), unroll=8)
        total = total + pltpu.roll(total, HALF, axis=1)
        mean_send2[chunk] = total
        mean_recv2[chunk, me] = total
        exchange(lambda other: mean_send2.at[chunk], lambda mine: mean_recv2.at[chunk, mine],
                 sem_small_out.at[4 + chunk], sem_small_in.at[4 + chunk])

    def write_averages():
        await_bytes(mean_recv.at[pl.ds(0, GROUPS - 1)], sem_small_in.at[2])
        for f in range(FIELDS):
            for k in range(4):
                averages[0, f, 2 * k:2 * k + 2] = mean_recv[4 * f + k]
        for chunk in range(CHUNKS):
            await_bytes(others(mean_recv2, chunk), sem_small_in.at[4 + chunk])
            for f in range(PAIR):
                def loader(g):
                    return lambda u: mean_recv2[chunk, STRIPS * f + g]

                spans = [(WIDE * g, EDGE, WIDE, loader(g), LANES) for g in range(STRIPS)]
                for u in range(COLS // LANES):
                    averages[1, PAIR * chunk + f, :, LANES * u:LANES * (u + 1)] = place(u, spans)

    def edge_coefficients():
        for m in range(2):
            raw[m] = half_turn(courant_v[m])
        for f in range(FIELDS):
            raw[2 + f] = half_turn(diffusion_v[f])

    def coefficients(field):
        def sixteen(m):
            mid = raw[m]
            return jnp.concatenate([jnp.where(upper, raw_north[m], mid), jnp.where(upper, mid, raw_south[m])], axis=0)

        inside = jnp.concatenate([jnp.where(upper, has_north, 1.0), jnp.where(upper, 1.0, has_south)], axis=0)
        column2 = jnp.concatenate([column, column], axis=0)
        cx, cy, d = sixteen(0), sixteen(1), sixteen(2 + field)
        coef[field, 0] = inside * (1.0 - jnp.abs(cx) - jnp.abs(cy) - 4.0 * d)
        coef[field, 1] = inside * (jnp.maximum(cx, 0.0) + d)
        coef[field, 2] = inside * (d - jnp.minimum(cx, 0.0))
        coef[field, 3] = jnp.where(column2 > 0, inside * (jnp.maximum(cy, 0.0) + d), 0.0)
        coef[field, 4] = jnp.where(column2 < COLS - 1, inside * (d - jnp.minimum(cy, 0.0)), 0.0)

    def window(get, rows):
        for g in range(STRIPS):
            spans = [(HALF * h, WIDE * g - EDGE, SPAN, lambda u: get(pl.ds(LANES * u, LANES)), COLS) for h in range(2)]
            windows[g, :rows] = place(0, spans, rows)
        return windows[strip, :rows]

    def coefficients2(chunk):
        lane16 = lax.broadcasted_iota(jnp.int32, (2 * ROWS, LANES), 1)
        used = lax.rem(lane16, HALF) < SPAN
        for n in range(5):
            here = window(lambda cols: coef[PAIR * chunk + in_pair, n, :, cols], 2 * ROWS)
            coef2[chunk, n] = jnp.where(used, here, 0.0)

    def observations():
        cell = lax.broadcasted_iota(jnp.int32, (ROWS, COLS), 0) * COLS + column
        zero = jnp.zeros((ROWS, COLS), jnp.float32)

        def gather(k, sums):
            here = cell == obs_loc_s[0, k]
            precision = jnp.where(here, 1.0 / jnp.full((1, COLS), obs_var_s[0, k], jnp.float32), 0.0)
            return (sums[0] + precision,) + tuple(sums[1 + c] + precision * observed_s[c, 0, k] for c in range(CYCLES))

        sums = lax.fori_loop(0, NOBS, gather, (zero,) * (1 + CYCLES))
        obs_weight[...] = sums[0]
        seen = sums[0] > 0.0
        means = []
        for c in range(CYCLES):
            means.append(jnp.where(seen, sums[1 + c] / jnp.where(seen, sums[0], 1.0), 0.0))
            obs_mean[c] = means[c]

        def rest(k, sums):
            here = cell == obs_loc_s[0, k]
            precision = jnp.where(here, 1.0 / jnp.full((1, COLS), obs_var_s[0, k], jnp.float32), 0.0)
            return tuple(sums[c] + precision * (observed_s[c, 0, k] - means[c]) * (observed_s[c, 0, k] - means[c])
                         for c in range(CYCLES))

        sums = lax.fori_loop(0, NOBS, rest, (zero,) * CYCLES)
        for c in range(CYCLES):
            obs_rest[c] = sums[c]

    def observations2():
        inner = lax.rem(lane8, HALF)
        own = (inner >= EDGE) & (inner < EDGE + WIDE)
        first = jnp.where(in_pair == 0, 1.0, 0.0).astype(jnp.float32)
        obs2[0] = jnp.where(own, window(lambda cols: obs_weight[:, cols], ROWS), 0.0) * first
        obs2[1] = window(lambda cols: obs_mean[1, :, cols], ROWS)
        obs2[2] = jnp.where(own, window(lambda cols: obs_rest[1, :, cols], ROWS), 0.0) * first

    def noise_of(k, field, cols):
        return noise_v[1, k, field, :, cols]

    def state_of(k, field, cols):
        return result[field, k, :, cols]

    for n in (0, 1, 2, 6, 7):
        loads[n].wait()
    edge_coefficients()
    begin(0)
    begin(1)
    pl.semaphore_wait(barrier, GROUPS + 1)
    for way in (True, False):
        raw_copy(0, way).start()
    for f in range(2):
        for way in (True, False):
            halo_copy(f, way).start()
    pack(0, noise_of, noise_send, noise_recv)
    swap(noise_send, noise_recv, 0, 0)
    for n in (3, 4, 5, 8, 9, 10, 11):
        loads[n].wait()
    for f in range(2, FIELDS):
        begin(f)
        for way in (True, False):
            halo_copy(f, way).start()
    for way in (True, False):
        raw_copy(1, way).start()
    observations()
    for way in (True, False):
        raw_copy(0, way).wait_recv()
    coefficients(0)
    forecast(0)
    likelihood()
    for way in (True, False):
        raw_copy(1, way).wait_recv()
    coefficients(1)
    forecast(1)
    pack(0, state_of, state_send, state_recv)
    swap(state_send, state_recv, 0, 1)
    pack(1, noise_of, noise_send, noise_recv)
    swap(noise_send, noise_recv, 1, 0)
    for f in range(2, FIELDS):
        coefficients(f)
        forecast(f)
    pack(1, state_of, state_send, state_recv)
    swap(state_send, state_recv, 1, 1)
    weigh()
    average()
    for chunk in range(CHUNKS):
        coefficients2(chunk)
    observations2()
    unpack_noise(0)
    await_bytes(others(state_recv, 0), sem_in.at[0, 1])
    unpack_state(0)
    for block in range(BLOCKS):
        begin2(0, block)
    for block in range(BLOCKS):
        forecast2(0, block)
    likelihood2()
    pack_back(0)
    combine()
    unpack_noise(1)
    await_bytes(others(state_recv, 1), sem_in.at[1, 1])
    swap(back_send, back_recv, 0, 2)
    unpack_state(1)
    for block in range(BLOCKS):
        begin2(1, block)
    weigh2()
    average2(0)
    for block in range(BLOCKS):
        forecast2(1, block)
    pack_back(1)
    swap(back_send, back_recv, 1, 2)
    average2(1)
    finish(0)
    finish(1)
    write_averages()
    for chunk in range(CHUNKS):
        store(chunk).wait()
        for which, ref in enumerate((noise_recv, state_recv, back_recv)):
            await_bytes(others(ref, chunk), sem_out.at[chunk, which])
        await_bytes(others(mean_recv2, chunk), sem_small_out.at[4 + chunk])
    for way in (True, False):
        for f in range(FIELDS):
            halo_copy(f, way).wait_send()
        for part in range(2):
            raw_copy(part, way).wait_send()
        for chunk in range(CHUNKS):
            for block in range(BLOCKS):
                halo_copy2(chunk, block, way).wait_send()
    for n, ref in enumerate((like_recv, part_recv, mean_recv, like_recv2)):
        await_bytes(ref.at[pl.ds(0, GROUPS - 1)], sem_small_out.at[n])


def per_device(members, noise, courant, diffusion, obs_loc, observed, obs_var, ancestors):
    f32 = jnp.float32
    anywhere = pl.BlockSpec(memory_space=pl.ANY)
    plane = (ROWS, COLS)
    one = (ROWS, LANES)
    operands = (members, noise, courant, diffusion, obs_loc, observed, obs_var, ancestors)

    def vmem(*shape):
        return pltpu.VMEM(shape, f32)

    scratch = [vmem(*a.shape) for a in operands[:4]] + [pltpu.SMEM(a.shape, a.dtype) for a in operands[4:]]
    scratch += [vmem(PER, FIELDS, *plane)]
    scratch += [vmem(CHUNKS, GROUPS, ROWS, PER * SPAN) for _ in range(4)]
    scratch += [vmem(CHUNKS, GROUPS, ROWS, PER * WIDE) for _ in range(2)]
    scratch += [vmem(FIELDS, PER // 2, *plane) for _ in range(4)]
    scratch += [vmem(CHUNKS, PAIRS // 2, *one) for _ in range(4)]
    scratch += [
        vmem(FIELDS, PER, *plane),
        vmem(FIELDS, PER, *plane),
        vmem(2 + FIELDS, *plane),
        vmem(2 + FIELDS, *plane),
        vmem(2 + FIELDS, *plane),
        vmem(FIELDS, 5, 2 * ROWS, COLS),
        vmem(*plane),
        vmem(CYCLES, *plane),
        vmem(CYCLES, *plane),
        vmem(PER, LANES),
        vmem(PER, LANES),
        vmem(PER, LANES),
        vmem(1, LANES),
        vmem(GROUPS, 1, LANES),
        vmem(GROUPS, 2, COLS),
        vmem(GROUPS, 2, COLS),
        vmem(2, COLS),
        vmem(GROUPS, 2, COLS),
        vmem(CHUNKS, PAIRS, *one),
        vmem(CHUNKS, ALL, *one),
        vmem(CHUNKS, PAIRS, *one),
        vmem(CHUNKS, ALL, *one),
        vmem(CHUNKS, 5, 2 * ROWS, LANES),
        vmem(STRIPS, 2 * ROWS, LANES),
        vmem(3, *one),
        vmem(PAIRS, LANES),
        vmem(PAIRS, LANES),
        vmem(PAIRS, LANES),
        vmem(2, LANES),
        vmem(GROUPS, 2, LANES),
        vmem(CHUNKS, *one),
        vmem(CHUNKS, GROUPS, *one),
        pltpu.SemaphoreType.DMA((12,)),
        pltpu.SemaphoreType.DMA((CHUNKS,)),
        pltpu.SemaphoreType.DMA((CHUNKS, 3)),
        pltpu.SemaphoreType.DMA((CHUNKS, 3)),
        pltpu.SemaphoreType.DMA((FIELDS, 2)),
        pltpu.SemaphoreType.DMA((FIELDS, 2)),
        pltpu.SemaphoreType.DMA((CHUNKS, BLOCKS, 2)),
        pltpu.SemaphoreType.DMA((CHUNKS, BLOCKS, 2)),
        pltpu.SemaphoreType.DMA((2, 2)),
        pltpu.SemaphoreType.DMA((2, 2)),
        pltpu.SemaphoreType.DMA((6,)),
        pltpu.SemaphoreType.DMA((6,)),
    ]
    return pl.pallas_call(
        kernel,
        out_shape=(
            jax.ShapeDtypeStruct((PER, FIELDS) + plane, f32),
            jax.ShapeDtypeStruct((CYCLES, FIELDS) + plane, f32),
        ),
        in_specs=[anywhere] * 8,
        out_specs=(anywhere, pl.BlockSpec(memory_space=pltpu.VMEM)),
        scratch_shapes=scratch,
        compiler_params=pltpu.CompilerParams(
            collective_id=0, has_side_effects=True, vmem_limit_bytes=60 * 1024 * 1024
        ),
        name="assimilate",
    )(*operands)


def solution(mesh):
    return jax.shard_map(
        per_device,
        mesh=mesh,
        in_specs=(
            P("dom", None, "tile", None),
            P(None, "dom", None, "tile", None),
            P(None, "tile", None),
            P(None, "tile", None),
            P("tile", None),
            P(None, "tile", None),
            P("tile", None),
            P(None, "tile", None),
        ),
        out_specs=(P("dom", None, "tile", None), P(None, None, "tile", None)),
        check_vma=False,
    )
```

time: 453 us -> 104 us (0.23)
  waiting for transfers between devices: 295 us -> 0 us
  Pallas kernels: 0 us -> 101 us
  blocking collectives: 52.9 us -> 0 us
  starting transfers between devices: 41.2 us -> 0 us
  other arithmetic: 26 us -> 0 us
  local copies, waits for them, and re-layouts: 18.4 us -> 2.75 us
  between operations: 14.3 us -> 0.65 us
    all_gather x2 -> x0, waiting for transfers between devices: 162 us -> none  [per_device(): gathered = lax.all_gather(fields, 'dom', axis=0, tiled=True)]
    psum x1 -> x0, waiting for transfers between devices: 103 us -> none  [per_device(): averages.append(lax.psum(local_average, 'dom'))]
    pallas_call x0 -> x1, Pallas kernels: none -> 101 us  [per_device(): pl.pallas_call(kernel, out_shape=(jax.ShapeDtypeStruct((PER, FIELDS) + pl...]
    ppermute x16 -> x0, starting transfers between devices: 41.1 us -> none  [the longest x8 30.6 us: padded_2(): lax.ppermute(lax.slice_in_dim(block, block.shape[dim] - width, None, axis...]
    ppermute x16 -> x0, waiting for transfers between devices: 29.1 us -> none  [the longest x8 26.9 us: padded_2(): lax.ppermute(lax.slice_in_dim(block, 0, width, axis=dim), axis, backward)]
    pmax x1 -> x0, blocking collectives: 28.7 us -> none  [per_device(): peak_value = lax.pmax(jnp.max(log_likelihood), 'dom')]
    psum x1 -> x0, blocking collectives: 24.2 us -> none  [per_device(): lax.psum(jnp.sum(jnp.exp(log_likelihood - peak_value)), 'dom')]
    gather x4 -> x0, local copies, waits for them, and re-layouts: 13.8 us -> none  [the longest x2 11.2 us: per_device(): fields = gathered[mine_lineage]]
  transfers between devices with their start and end apart: 19 -> 0, of which waited for: 18 -> 0; matrix products, arithmetic and copies ran while one was open for 1% -> 0% of each run, Pallas kernels for 0% -> 0%
where the time goes in v1:
time: 104 us
  Pallas kernels  101 us (97%)
  local copies, waits for them, and re-layouts  2.75 us (3%)
    pallas_call x1, Pallas kernels, per_device(): pl.pallas_call(kernel, out_shape=(jax.ShapeDtypeStruct((PER, FIELDS) + pl...  101 us
    unnamed x4, local copies, waits for them, and re-layouts  2.75 us

profile of v1, /device:TPU:1, one launch (start us, length us, event | category | flops | bytes accessed | tf_op | source)
XLA Modules:
  0.0 103.9 jit_solution(8118065478954348604)
XLA Ops:
  0.6 100.5 %assimilate.1 = (f32[16,4,8,384]{3,2,1,0:T(8,128)}, f32[2,4,8,384]{3,2,1,0:T(8,128)}) custom-call(f32[16,4,8,384]{3,2,1,0:T(8,128)} %members.1, f32[2,16,4,8,384]{4,3,2,1,0:T(8,128)} %noise.1, f32[2,8,384]{2,1,0:T(8,128)} %courant.1, f32[4,8,384]{2,1,0:T(8,128)} %diffusion.1, s32[1,64]{1,0:T(1,128)} %obs_loc.1, f32[2,1,64]{2,1,0:T(1,128)} %observed.1, ...), custom_call_target="tpu_custom_call" | custom-call | tf_op jit(solution)/shard_map/assimilate/pallas_call | solution.py:636
  101.2 0.0 copy-start
  101.2 2.1 %copy.12 = f32[16,4,8,384]{3,2,1,0:T(8,128)} copy(f32[16,4,8,384]{3,2,1,0:T(8,128)} %get-tuple-element.4) | data formatting | bytes 1572864
  103.3 0.0 copy-done
  103.3 0.6 copy.13
Async XLA Ops:
  101.2 2.1 %copy-start = (f32[2,4,8,384]{3,2,1,0:T(8,128)S(1)}, f32[2,4,8,384]{3,2,1,0:T(8,128)}, u32[]{:S(2)}) copy-start(f32[2,4,8,384]{3,2,1,0:T(8,128)} %get-tuple-element.5) | copy-start | bytes 294916
